TPU v7x, 32 devices: a whole 2x2x4 slice. The times are simulated.
32 devices in a mesh: grp: 2 (over x), pole: 4 (over z), row: 4 (over y, core).
Axes of the slice: x: 2, y: 2, z: 4, core: 2. Of those that a mesh axis runs over, the one named last changes fastest.
Arguments:
- aux_modes: float32 [64, 2, 3072, 128], P(('grp', 'pole'), None, 'row'), parts along dimension 0, may hold values from -6 to 6
- rho_panel: float32 [2, 6144, 256], P(None, ('grp', 'row')), parts along dimension 1, may hold values from -6 to 6
- ham_blocks: float32 [48, 5, 2, 128, 128], P(('grp', 'row')), parts along dimension 0, may hold values from -0.25 to 0.25
- block_counts: int32 [48], P(('grp', 'row')), parts along dimension 0, may hold values from 1 to 5, as said below
- block_offsets: int32 [48, 5], P(('grp', 'row')), parts along dimension 0, may hold values from -2 to 2, as said below
- lead_gamma: float32 [2, 2, 128, 128], replicated, may hold values from -0.5 to 0.5
- pole_energy: float32 [2, 64], P(None, ('grp', 'pole')), parts along dimension 1, may hold values from -1 to 1
- residues: float32 [2, 64], P(None, ('grp', 'pole')), parts along dimension 1, may hold values from -1.2 to 1.2
- pole_lead: int32 [64], P(('grp', 'pole')), parts along dimension 0, may hold values from 0 to 1, as said below
Outputs:
- slopes: float32 [64, 2, 3072, 128], P(('grp', 'pole'), None, 'row'), parts along dimension 0
- lead_term: float32 [2, 6144, 256], P(None, ('grp', 'row')), parts along dimension 1
There are 2 independent parts, one for each index of `grp`. A program takes and returns all parts, laid end to end along the dimension named above; an argument that names none is the same for every part. Nothing has to cross between parts.
Inputs may be any that keep to these rules, and one draw needn't show every extreme that they name: `block_counts`: some row block uses all 5 slots and some only one. `block_offsets`: slot 0 of every row block is 0; the 5 entries of a row block are distinct. `pole_lead`: each lead has exactly 16 poles.
All inputs are finite; a program needn't handle non-finite values.
Results may differ from a plain program's by a relative error of at most 0.0003.
Values sent between devices are 32-bit elements; how exact they have to be, the bound alone decides.
No kernel may reach another device: no remote copies, remote signals or barrier semaphores. Data moves between devices by JAX's collectives and lax.ppermute only.
A program may use at most 128 MiB of HBM per device.

v0:
```python
import functools

import jax
import jax.numpy as jnp
from jax import lax
from jax.experimental import pallas as pl
from jax.experimental.pallas import tpu as pltpu
from jax.sharding import PartitionSpec as P

REACH = 2
CHUNKS = 3
F32 = jnp.float32
BF16 = jnp.bfloat16
MIB = 2**20
LIMIT = 6
BIG = 10**10
COSTS = {("add", 1, 0): BIG, ("finish", 0): BIG}
SMEM_SPEC = pl.BlockSpec(memory_space=pltpu.SMEM)
VMEM_SPEC = pl.BlockSpec(memory_space=pltpu.VMEM)
ANY_SPEC = pl.BlockSpec(memory_space=pl.ANY)


def dot(left, right):
    return jnp.dot(left, right, preferred_element_type=F32)


def split_high_low(value):
    high = value.astype(BF16)
    return high, (value - high.astype(F32)).astype(BF16)


def kept(value, place):
    spaces = {"vmem": pltpu.VMEM, "hbm": pltpu.HBM, "smem": pltpu.HBM}
    return pltpu.with_memory_space_constraint(value, spaces[place]) if place in spaces else value


def call(kernel, name, operands, outputs, after=(), scratch=(), aliases=None, through=(), cost=0, limit=LIMIT):
    places = {"smem": SMEM_SPEC, "vmem": VMEM_SPEC, "any": ANY_SPEC, "hbm": ANY_SPEC}
    arrays = [kept(a, place) for a, place in operands]
    passed = [kept(a, place) for a, place in through]
    specs = [places[place] for _, place in operands]
    count = len(operands)
    skipped = len(through) + len(after)
    aliases = dict(aliases or {})
    for i in range(len(through)):
        aliases[count + i] = len(outputs) + i

    def body(*refs):
        refs, outs = refs[:count], refs[count + skipped :]
        kernel(*refs, *outs[: len(outputs)], *outs[len(outputs) + len(through) + 1 :])

    shapes = [
        {"vmem": pltpu.VMEM, "hbm": pltpu.HBM}.get(place, jax.ShapeDtypeStruct)(shape, dtype)
        for shape, dtype, place in [*outputs, *((a.shape, a.dtype, place) for a, place in through)]
    ]
    result = pl.pallas_call(
        body,
        in_specs=specs + [places[place] for _, place in through] + [ANY_SPEC] * len(after),
        out_specs=[places[place] for _, _, place in outputs] + [places[place] for _, place in through] + [ANY_SPEC],
        out_shape=shapes + [jax.ShapeDtypeStruct((8, 128), F32)],
        scratch_shapes=list(scratch),
        input_output_aliases=aliases,
        compiler_params=pltpu.CompilerParams(vmem_limit_bytes=limit * MIB),
        cost_estimate=pl.CostEstimate(flops=cost, bytes_accessed=cost, transcendentals=0),
        name=name,
    )(*arrays, *passed, *after)
    return list(result[:-1]), result[-1]


def mix_tile(lead_ref, residue_ref, load, store, poles, width):
    sums = [None] * 4
    for pole in range(poles):
        real, imag = load(pole)
        for lead in range(2):
            alive = (lead_ref[pole] == lead).astype(F32)
            coef_real = alive * residue_ref[0, pole]
            coef_imag = alive * residue_ref[1, pole]
            terms = (
                coef_real * real - coef_imag * imag,
                coef_real * imag + coef_imag * real,
            )
            for part in range(2):
                slot = 2 * part + lead
                sums[slot] = terms[part] if pole == 0 else sums[slot] + terms[part]
    for part in range(2):
        for lead in range(2):
            store(part, slice(lead * width, (lead + 1) * width), sums[2 * part + lead])


def mix_range(lead_ref, residue_ref, aux_ref, out_ref, aux_start, out_start, rows, tile=32):
    poles = aux_ref.shape[0]
    width = aux_ref.shape[-1]
    tile = next(t for t in (tile, 16, 8) if rows % t == 0)

    def step(i, carry):
        at = pl.ds(pl.multiple_of(aux_start + i * tile, 8), tile)
        to = pl.ds(pl.multiple_of(out_start + i * tile, 8), tile)

        def load(pole):
            return aux_ref[pole, 0, at, :], aux_ref[pole, 1, at, :]

        def store(part, columns, value):
            out_ref[part, to, columns] = value

        mix_tile(lead_ref, residue_ref, load, store, poles, width)
        return carry

    lax.fori_loop(0, rows // tile, step, 0)


def first_kernel(first, last, sends_ref, lead_ref, residue_ref, aux_ref, out_ref, mode_ref, sems):
    pieces = 4
    size = (last - first) // pieces
    copies = [
        pltpu.make_async_copy(
            aux_ref.at[:, :, pl.ds(first + i * size, size), :],
            mode_ref.at[:, :, pl.ds(i * size, size), :],
            sems.at[i],
        )
        for i in range(pieces)
    ]

    @pl.when(sends_ref[0] == 1)
    def _():
        for copy in copies:
            copy.start()
        for i, copy in enumerate(copies):
            copy.wait()
            mix_range(lead_ref, residue_ref, mode_ref, out_ref, i * size, i * size, size)


def later_kernel(ranges, lead_ref, residue_ref, odd_ref, gamma_ref, aux_ref, *rest):
    outs = rest[: len(ranges)]
    near_ref, far_ref, ghigh_ref, glow_ref, mode_ref, sems, edge_sems = rest[len(ranges) :]
    rows = aux_ref.shape[2]
    halo = near_ref.shape[2]
    copies = []
    place = 0
    places = []
    for i, (first, last) in enumerate(ranges):
        at = pl.ds(first, last - first)
        to = pl.ds(place, last - first)
        copies.append(pltpu.make_async_copy(aux_ref.at[:, :, at, :], mode_ref.at[:, :, to, :], sems.at[i]))
        places.append(place)
        place += last - first
    order = [*range(1, len(ranges)), 0]
    for i in order:
        copies[i].start()
    for lead in range(2):
        gamma_real = gamma_ref[lead, 0]
        gamma_imag = gamma_ref[lead, 1]
        gamma = jnp.concatenate(
            [
                jnp.concatenate([gamma_real, gamma_imag], axis=1),
                jnp.concatenate([-gamma_imag, gamma_real], axis=1),
            ],
            axis=0,
        )
        ghigh_ref[lead], glow_ref[lead] = split_high_low(gamma)
    odd = odd_ref[0]
    held = [(0, halo), (rows - halo, rows)]
    whole = all(side in ranges for side in held)
    sides = ((0, 1 - odd), (rows - halo, odd))
    edges = []
    for i, (start, side) in enumerate(sides):
        if whole:
            copies[ranges.index(held[i])].wait()
            source = mode_ref.at[:, :, pl.ds(places[ranges.index(held[i])], halo), :]
        else:
            source = aux_ref.at[:, :, pl.ds(start, halo), :]
        for j, ref in enumerate((near_ref, far_ref)):
            edge = pltpu.make_async_copy(source, ref, edge_sems.at[j])
            pl.when(side == j)(edge.start)
        edges.append(pltpu.make_async_copy(source, near_ref, edge_sems.at[i]))
    for i in order:
        first, last = ranges[i]
        if not (whole and ranges[i] in held):
            copies[i].wait()
        mix_range(lead_ref, residue_ref, mode_ref, outs[i], places[i], 0, last - first)
    for edge in edges:
        edge.wait()


def add_kernel(left_ref, right_ref, out_ref):
    out_ref[...] = left_ref[...] + right_ref[...]


def pair_split(ham_ref, index, which):
    ham_real = ham_ref[index, which, 0]
    ham_imag = ham_ref[index, which, 1]
    pair = jnp.concatenate(
        [
            jnp.concatenate([ham_real, -ham_imag], axis=1),
            jnp.concatenate([ham_imag, ham_real], axis=1),
        ],
        axis=0,
    )
    return split_high_low(pair)


def product(ham_ref, index, which, mode_ref, place, rows, high_ref, low_ref):
    poles = mode_ref.shape[-4]
    width = mode_ref.shape[-1]
    for pole in range(poles):
        for part in range(2):
            high, low = split_high_low(mode_ref[place, pole, part, rows, :])
            where = (pl.ds(part * width, width), pl.ds(pole * width, width))
            high_ref[where] = high
            low_ref[where] = low
    pair_high, pair_low = pair_split(ham_ref, index, which)
    return dot(pair_high, high_ref[...]) + dot(pair_high, low_ref[...]) + dot(pair_low, high_ref[...])


def ham_kernel(first, last, count_ref, offset_ref, energy_ref, ham_ref, aux_ref, out_ref, blocks_ref, mode_ref, high_ref, low_ref, total_ref, ham_sems, mode_sems):
    poles, _, rows, width = aux_ref.shape
    nblock = rows // width
    slots = ham_ref.shape[1]
    base = max(first - REACH, 0)
    ending = min(last + REACH, nblock)
    own = range(first, last)
    others = [block for block in range(base, ending) if block not in own]
    heads = []
    tails = []
    for i, row in enumerate(own):
        heads.append(pltpu.make_async_copy(ham_ref.at[row, 0], blocks_ref.at[i, 0], ham_sems.at[i, 0]))
        rest = pl.ds(1, slots - 1)
        tails.append(pltpu.make_async_copy(ham_ref.at[row, rest], blocks_ref.at[i, rest], ham_sems.at[i, 1]))
    mode_copies = {
        block: pltpu.make_async_copy(
            aux_ref.at[:, :, pl.ds(block * width, width), :], mode_ref.at[block - base], mode_sems.at[block - base]
        )
        for block in range(base, ending)
    }
    for i, row in enumerate(own):
        heads[i].start()
        mode_copies[row].start()
    for i, row in enumerate(own):
        pl.when(count_ref[row] > 1)(tails[i].start)
    needed = {}
    for block in others:
        uses = [
            (which < count_ref[row]) & (row + offset_ref[row, which] == block)
            for row in own
            for which in range(1, slots)
        ]
        needed[block] = functools.reduce(jnp.logical_or, uses)
        pl.when(needed[block])(mode_copies[block].start)
    whole = pl.ds(0, width)
    for i, row in enumerate(own):
        heads[i].wait()
        mode_copies[row].wait()
        total_ref[i] = product(blocks_ref, i, 0, mode_ref, row - base, whole, high_ref, low_ref)
    for i, row in enumerate(own):
        pl.when(count_ref[row] > 1)(tails[i].wait)
    for block in others:
        pl.when(needed[block])(mode_copies[block].wait)
    for i, row in enumerate(own):

        def slot(which, carry):
            place = row + offset_ref[row, which]

            @pl.when((place >= 0) & (place < nblock))
            def _():
                total_ref[i] += product(blocks_ref, i, which, mode_ref, place - base, whole, high_ref, low_ref)

            return carry

        lax.fori_loop(1, count_ref[row], slot, 0)
        for pole in range(poles):
            real = mode_ref[row - base, pole, 0]
            imag = mode_ref[row - base, pole, 1]
            energy_real = energy_ref[0, pole]
            energy_imag = energy_ref[1, pole]
            columns = slice(pole * width, (pole + 1) * width)
            at = pl.ds(i * width, width)
            out_ref[pole, 0, at, :] = total_ref[i, width:, columns] - (energy_real * imag + energy_imag * real)
            out_ref[pole, 1, at, :] = (energy_real * real - energy_imag * imag) - total_ref[i, :width, columns]


def ham_part(first, last, aux_modes, ham_blocks, block_counts, block_offsets, pole_energy, after, cost):
    poles, _, rows, width = aux_modes.shape
    nblock, slots = ham_blocks.shape[:2]
    n = last - first
    held = min(last + REACH, nblock) - max(first - REACH, 0)
    (slopes,), token = call(
        functools.partial(ham_kernel, first, last),
        "ham",
        [
            (block_counts, "smem"), (block_offsets, "smem"), (pole_energy, "smem"),
            (ham_blocks, "hbm"), (aux_modes, "hbm"),
        ],
        [((poles, 2, n * width, width), F32, "vmem")], after,
        scratch=[
            pltpu.VMEM((n, slots, 2, width, width), F32),
            pltpu.VMEM((held, poles, 2, width, width), F32),
            pltpu.VMEM((2 * width, poles * width), BF16),
            pltpu.VMEM((2 * width, poles * width), BF16),
            pltpu.VMEM((n, 2 * width, poles * width), F32),
            pltpu.SemaphoreType.DMA((n, 2)),
            pltpu.SemaphoreType.DMA((held,)),
        ],
        cost=cost,
        limit=14,
    )
    return slopes, token


def edge_kernel(nblock, bounds, count_ref, offset_ref, odd_ref, ham_ref, near_ref, far_ref, *refs):
    pieces = len(bounds)
    ins, outs = refs[:pieces], refs[pieces : 2 * pieces]
    blocks_ref, high_ref, low_ref, total_ref, ham_sems = refs[2 * pieces :]
    poles = near_ref.shape[1]
    width = near_ref.shape[-1]
    odd = odd_ref[0]
    edge_rows = list(range(REACH)) + list(range(nblock - REACH, nblock))
    ham_copies = [
        pltpu.make_async_copy(ham_ref.at[row], blocks_ref.at[i], ham_sems.at[i]) for i, row in enumerate(edge_rows)
    ]
    for copy in ham_copies:
        copy.start()
    for in_ref, out_ref in zip(ins, outs):
        out_ref[...] = in_ref[...]
    for i, row in enumerate(edge_rows):
        out_ref, at = next(
            (ref, pl.ds((row - a) * width, width)) for ref, (a, b) in zip(outs, bounds) if a <= row < b
        )
        ham_copies[i].wait()

        def slot(which, carry):
            place = row + offset_ref[row, which]
            below = place < 0
            above = place >= nblock
            start = pl.multiple_of(jnp.where(below, place + REACH, place - nblock) * width, width)

            def add(halo_ref):
                total_ref[...] = product(blocks_ref, i, which, halo_ref, 0, pl.ds(start, width), high_ref, low_ref)
                for pole in range(poles):
                    columns = slice(pole * width, (pole + 1) * width)
                    out_ref[pole, 0, at, :] += total_ref[width:, columns]
                    out_ref[pole, 1, at, :] -= total_ref[:width, columns]

            pl.when((below & (odd == 1)) | (above & (odd == 0)))(lambda: add(near_ref))
            pl.when((below & (odd == 0)) | (above & (odd == 1)))(lambda: add(far_ref))
            return carry

        lax.fori_loop(1, count_ref[row], slot, 0)


def edge_part(slopes, bounds, near, far, odd, ham_blocks, block_counts, block_offsets, after):
    nblock, slots = ham_blocks.shape[:2]
    poles, _, _, width = near.shape
    reached = [i for i, (a, b) in enumerate(bounds) if a < REACH or b > nblock - REACH]
    outs, token = call(
        functools.partial(edge_kernel, nblock, [bounds[i] for i in reached]), "edge",
        [
            (block_counts, "smem"), (block_offsets, "smem"), (odd, "smem"), (ham_blocks, "hbm"),
            (near[None], "vmem"), (far[None], "vmem"),
        ]
        + [(slopes[i], "vmem") for i in reached],
        [(slopes[i].shape, F32, "vmem") for i in reached], after,
        scratch=[
            pltpu.VMEM((2 * REACH, slots, 2, width, width), F32),
            pltpu.VMEM((2 * width, poles * width), BF16),
            pltpu.VMEM((2 * width, poles * width), BF16),
            pltpu.VMEM((2 * width, poles * width), F32),
            pltpu.SemaphoreType.DMA((2 * REACH,)),
        ],
        limit=8,
    )
    slopes = list(slopes)
    for i, out in zip(reached, outs):
        slopes[i] = out
    return slopes, token


def finish_kernel(first, starts, chained, *refs):
    lead_ref, taken_ref, ghigh_ref, glow_ref, rho_ref, local_ref, received_ref = refs[:7]
    slope_refs = refs[7 : 7 + len(starts)]
    refs = refs[7 + len(starts) + (2 if chained else 0) :]
    out_ref, lead_out_ref, wide_ref, source_ref, panel_ref, sems = refs
    poles, _, _, width = slope_refs[0].shape
    rows = local_ref.shape[1]
    at = pl.ds(first, rows)
    lead_term = jnp.where(taken_ref[0] == 1, received_ref[...], local_ref[...])
    wide_ref[...] = lead_term
    copies = [pltpu.make_async_copy(wide_ref, lead_out_ref.at[:, at, :], sems.at[poles])]
    copies[0].start()
    for lead in range(2):
        columns = slice(lead * width, (lead + 1) * width)
        pair = jnp.concatenate(
            [
                rho_ref[part, at, columns] + 0.25 * wide_ref[part, :, columns]
                for part in range(2)
            ],
            axis=1,
        )
        high, low = split_high_low(pair)
        source_ref[lead] = (
            dot(high, ghigh_ref[lead]) + dot(high, glow_ref[lead]) + dot(low, ghigh_ref[lead])
        )
    for pole in range(poles):
        lead = lead_ref[pole]
        for slope_ref, start in zip(slope_refs, starts):
            low_row = max(start, first)
            high_row = min(start + slope_ref.shape[2], first + rows)
            from_ = pl.ds(low_row - start, high_row - low_row)
            to = pl.ds(low_row - first, high_row - low_row)
            panel_ref[pole, 0, to, :] = slope_ref[pole, 0, from_, :] + source_ref[lead, to, width:]
            panel_ref[pole, 1, to, :] = slope_ref[pole, 1, from_, :] - source_ref[lead, to, :width]
        copies.append(
            pltpu.make_async_copy(panel_ref.at[pole], out_ref.at[pole, :, at, :], sems.at[pole])
        )
        copies[-1].start()
    for copy in copies:
        copy.wait()


def finish_rows(
    first, slopes, pieces, local, received, taken, rho_panel, ghigh, glow, pole_lead, results, out_shape, after, cost
):
    poles, _, _, width = out_shape
    rows = local.shape[1]
    starts = []
    touched = []
    for piece, (a, b) in zip(slopes, pieces):
        if a * width < first + rows and b * width > first:
            starts.append(a * width)
            touched.append((piece, "vmem"))
    operands = [
        (pole_lead, "smem"), (taken, "smem"), (ghigh, "vmem"), (glow, "vmem"), (rho_panel, "vmem"),
        (local, "vmem"), (received, "vmem"), *touched,
    ]
    aliases = None
    if results is not None:
        aliases = {len(operands) + i: i for i in range(2)}
        operands += [(result, "any") for result in results]
    return call(
        functools.partial(finish_kernel, first, starts, results is not None),
        "finish", operands,
        [(out_shape, F32, "any"), (rho_panel.shape, F32, "any")], after,
        scratch=[
            pltpu.VMEM((2, rows, 2 * width), F32),
            pltpu.VMEM((2, rows, 2 * width), F32),
            pltpu.VMEM((poles, 2, rows, width), F32),
            pltpu.SemaphoreType.DMA((poles + 1,)),
        ],
        aliases=aliases,
        cost=cost,
    )


def per_device(
    aux_modes,
    rho_panel,
    ham_blocks,
    block_counts,
    block_offsets,
    lead_gamma,
    pole_energy,
    residues,
    pole_lead,
):
    poles, _, rows, width = aux_modes.shape
    nblock = rows // width
    halo = REACH * width
    devices = lax.axis_size("row")
    odd = (lax.axis_index("row") % 2).astype(jnp.int32).reshape(1)
    count = lax.axis_size("pole")
    me = lax.axis_index("pole")
    inner = count // 2 - 1
    line = count % 2 == 0 and count >= 4

    taken = ((me == 0) | (me == count - 1)).astype(jnp.int32).reshape(1)
    sends = taken if line else jnp.ones_like(taken)

    chunks = CHUNKS
    ranges = [(c * rows // chunks, (c + 1) * rows // chunks) for c in range(chunks)]
    ranges = [ranges[1], ranges[0], *ranges[2:]]
    sizes = [b - a for a, b in ranges]

    (part,), token = call(
        functools.partial(first_kernel, *ranges[0]), "mix",
        [(sends, "smem"), (pole_lead, "smem"), (residues, "smem"), (aux_modes, "hbm")],
        [((2, sizes[0], 2 * width), F32, "vmem")],
        scratch=[pltpu.VMEM((poles, 2, sizes[0], width), F32), pltpu.SemaphoreType.DMA((4,))],
    )
    later, token = call(
        functools.partial(later_kernel, ranges), "mix_later",
        [(pole_lead, "smem"), (residues, "smem"), (odd, "smem"), (lead_gamma, "vmem"), (aux_modes, "hbm")],
        [((2, size, 2 * width), F32, "vmem") for size in sizes]
        + [((poles, 2, halo, width), F32, "hbm")] * 2
        + [((2, 2 * width, 2 * width), BF16, "vmem")] * 2,
        [token],
        scratch=[
            pltpu.VMEM(aux_modes.shape, F32),
            pltpu.SemaphoreType.DMA((chunks,)),
            pltpu.SemaphoreType.DMA((2,)),
        ],
        limit=8,
    )
    near_edge, far_edge, ghigh, glow = later[chunks:]
    locals_ = later[:chunks]

    near_pairs = [(i, i + 1) for i in range(0, devices - 1, 2)]
    far_pairs = [(i, i + 1) for i in range(1, devices - 1, 2)]
    received = [None] * chunks

    def fold_pairs(stage):
        if stage < inner:
            return [(stage, stage + 1), (count - 1 - stage, count - 2 - stage)]
        if stage == inner:
            return [(inner, inner + 1), (inner + 1, inner)]
        j = 2 * inner + 1 - stage
        return [(j, j - 1), (count - 1 - j, count - j)]

    def send(c, stage):
        if line:
            mine = part if c == stage == 0 else locals_[c]
            received[c] = lax.ppermute(mine, "pole", fold_pairs(stage))
        else:
            received[c] = lax.psum(locals_[c], "pole")

    def take(c, stage):
        nonlocal token
        if stage <= inner:
            (locals_[c],), token = call(
                add_kernel, "add", [(locals_[c], "vmem"), (received[c], "vmem")],
                [(locals_[c].shape, F32, "vmem")], [token], cost=COSTS.get(("add", c, stage), 0),
            )
        else:
            j = 2 * inner + 1 - stage
            target = (me == j - 1) | (me == count - j)
            locals_[c] = jnp.where(target, received[c], locals_[c])

    slopes = [None] * 3
    results = None
    pieces = [(i * nblock // 3, (i + 1) * nblock // 3) for i in range(3)]
    near = far = None

    def work(piece):
        nonlocal token
        slopes[piece], token = ham_part(
            *pieces[piece], aux_modes, ham_blocks, block_counts, block_offsets, pole_energy,
            [token], COSTS.get(("ham", piece), 0),
        )

    def neighbours():
        nonlocal near, far, token
        (near, far), token = call(
            lambda: None, "pass", [], [], [token], through=[(near_edge, "hbm"), (far_edge, "hbm")],
            cost=COSTS.get(("pass",), 0),
        )
        near = lax.ppermute(near, "row", near_pairs + [(b, a) for a, b in near_pairs])
        far = lax.ppermute(far, "row", far_pairs + [(b, a) for a, b in far_pairs])

    def reach():
        nonlocal slopes, token
        slopes, token = edge_part(
            slopes, pieces, near, far, odd, ham_blocks, block_counts, block_offsets, [token]
        )

    def finish(c):
        nonlocal results, token
        local = locals_[c] if line else received[c]
        results, token = finish_rows(
            ranges[c][0], slopes, pieces, local, received[c], taken, rho_panel, ghigh, glow, pole_lead,
            results, aux_modes.shape, [token], COSTS.get(("finish", c), 0),
        )

    for c in range(chunks):
        send(c, 0)
    for step in make_plan(line, 2 * inner, len(pieces)):
        if step[0] == "ham":
            work(step[1])
        elif step[0] == "edge":
            reach()
        elif step[0] == "pass":
            neighbours()
        elif step[0] == "finish":
            finish(step[1])
        else:
            take(*step)
            send(step[0], step[1] + 1)
    return tuple(results)


def make_plan(line, stages, pieces):
    work = [("ham", i) for i in [1, 0, *range(2, pieces)]]
    ending = [("edge",)] + [("finish", c) for c in range(1, CHUNKS)]
    plan = [work.pop(0)]
    if not line:
        return plan + [("pass",)] + work + [("finish", 0)] + ending
    for turn in range(CHUNKS + stages - 1):
        for stage in range(stages):
            if 0 <= turn - stage < CHUNKS:
                plan.append((turn - stage, stage))
            if turn == stage == 0:
                plan.append(("pass",))
        if turn == CHUNKS - 1:
            plan.append(("finish", 0))
        if turn > 0 and work:
            plan.append(work.pop(0))
    return plan + work + ending


def solution(mesh):
    placed = (
        P(("grp", "pole"), None, "row", None),
        P(None, ("grp", "row"), None),
        P(("grp", "row"), None, None, None, None),
        P(("grp", "row")),
        P(("grp", "row"), None),
        P(),
        P(None, ("grp", "pole")),
        P(None, ("grp", "pole")),
        P(("grp", "pole")),
    )
    return jax.shard_map(
        per_device,
        mesh=mesh,
        in_specs=placed,
        out_specs=(P(("grp", "pole"), None, "row", None), P(None, ("grp", "row"), None)),
        check_vma=False,
    )
```

profile of v0, /device:TPU:7, one launch (start us, length us, event | category | flops | bytes accessed | tf_op | source)
XLA Modules:
  0.0 76.8 jit_solution(9514797782795343095)
XLA Ops:
  0.7 2.6 %mix.1 = (f32[2,256,256]{2,1,0:T(8,128)S(1)}, f32[8,128]{1,0:T(8,128)S(1)}) custom-call(s32[1]{0:T(128)} %bitcast.refs_0_.refs_1_, s32[8]{0:T(128)} %refs_0_.15, f32[2,8]{1,0:T(2,128)} %refs_1_.7, f32[8,2,768,128]{3,2,1,0:T(8,128)} %refs_4_.11), custom_call_target="tpu_custom_call" | custom-call | tf_op jit(solution)/shard_map/mix/pallas_call | solution.py:56
  3.2 1.5 %collective-permute-start.1 = (f32[2,256,256]{2,1,0:T(8,128)S(1)}, f32[2,256,256]{2,1,0:T(8,128)S(1)}, u32[]{:S(2)}, u32[]{:S(2)}) collective-permute-start(f32[2,256,256]{2,1,0:T(8,128)S(1)} %get-tuple-element.49), channel_id=1, source_target_pairs={{0,4},{12,8},{1,5},{13,9},{2,6},{14,10},{3,7},{15,11},{16,20},{28,... | collective-permute-start | bytes 1572872 | tf_op jit(solution)/shard_map/ppermute | solution.py:519
  4.8 5.0 %mix_later.1 = (f32[2,256,256]{2,1,0:T(8,128)S(1)}, f32[2,256,256]{2,1,0:T(8,128)S(1)}, f32[2,256,256]{2,1,0:T(8,128)S(1)}, f32[8,2,256,128]{3,2,1,0:T(8,128)}, ...) custom-call(s32[8]{0:T(128)} %refs_0_.15, ...), custom_call_target="tpu_custom_call" | custom-call | tf_op jit(solution)/shard_map/mix_later/pallas_call | solution.py:56
  9.8 1.3 %collective-permute-start.3 = (f32[2,256,256]{2,1,0:T(8,128)S(1)}, f32[2,256,256]{2,1,0:T(8,128)S(1)}, u32[]{:S(2)}, u32[]{:S(2)}) collective-permute-start(f32[2,256,256]{2,1,0:T(8,128)S(1)} %get-tuple-element.53.refs_0_), channel_id=1, source_target_pairs={{0,4},{12,8},{1,5},{13,9},{2,6},{14,10},{3,7},{15,11},{16,20},{28,... | collective-permute-start | bytes 1572872 | tf_op jit(solution)/shard_map/ppermute | solution.py:519
  11.1 1.3 %collective-permute-start = (f32[2,256,256]{2,1,0:T(8,128)S(1)}, f32[2,256,256]{2,1,0:T(8,128)S(1)}, u32[]{:S(2)}, u32[]{:S(2)}) collective-permute-start(f32[2,256,256]{2,1,0:T(8,128)S(1)} %get-tuple-element.47.refs_0_), channel_id=1, source_target_pairs={{0,4},{12,8},{1,5},{13,9},{2,6},{14,10},{3,7},{15,11},{16,20},{28,... | collective-permute-start | bytes 1572872 | tf_op jit(solution)/shard_map/ppermute | solution.py:519
  12.4 9.1 %ham.3 = (f32[8,2,256,128]{3,2,1,0:T(8,128)S(1)}, f32[8,128]{1,0:T(8,128)S(1)}) custom-call(s32[6]{0:T(128)} %refs_0_.13, s32[6,5]{1,0:T(8,128)} %refs_1_.11, f32[2,8]{1,0:T(2,128)} %refs_2_.7, f32[6,5,2,128,128]{4,3,2,1,0:T(8,128)} %refs_3_.11, f32[8,2,768,128]{3,2,1,0:T(8,128)} %refs_4_.11, f32[8,128]{1,0:T(8,128)S(1)} %get-tuple-element.50.refs_5_), custom_call_target="tpu_custom_call" | custom-call | tf_op jit(solution)/shard_map/ham/pallas_call | solution.py:56
  21.6 0.7 collective-permute-start.2
  22.4 0.8 %collective-permute-start.9 = (f32[8,2,256,128]{3,2,1,0:T(8,128)}, f32[8,2,256,128]{3,2,1,0:T(8,128)S(1)}, u32[]{:S(2)}, u32[]{:S(2)}) collective-permute-start(f32[8,2,256,128]{3,2,1,0:T(8,128)} %get-tuple-element.71), channel_id=1, source_target_pairs={{1,2},{2,1},{5,6},{6,5},{9,10},{10,9},{13,14},{14,13},{17,18},{18,... | collective-permute-start | bytes 6291464 | tf_op jit(solution)/shard_map/ppermute | solution.py:554
  23.2 3.3 %collective-permute-done.3.refs_1_ = f32[2,256,256]{2,1,0:T(8,128)S(1)} collective-permute-done((f32[2,256,256]{2,1,0:T(8,128)S(1)}, f32[2,256,256]{2,1,0:T(8,128)S(1)}, u32[]{:S(2)}, u32[]{:S(2)}) %collective-permute-start.3) | collective-permute-done | bytes 524320 | tf_op jit(solution)/shard_map/ppermute | solution.py:519
  26.5 0.1 add.12
  26.6 0.7 collective-permute-start.6
  27.4 1.3 %collective-permute-start.5 = (f32[2,256,256]{2,1,0:T(8,128)S(1)}, f32[2,256,256]{2,1,0:T(8,128)S(1)}, u32[]{:S(2)}, u32[]{:S(2)}) collective-permute-start(f32[2,256,256]{2,1,0:T(8,128)S(1)} %get-tuple-element.62.refs_5_), channel_id=1, source_target_pairs={{4,0},{8,12},{5,1},{9,13},{6,2},{10,14},{7,3},{11,15},{20,16},{24,... | collective-permute-start | bytes 1572872 | tf_op jit(solution)/shard_map/ppermute | solution.py:519
  28.7 5.3 %ham.4 = (f32[8,2,256,128]{3,2,1,0:T(8,128)S(1)}, f32[8,128]{1,0:T(8,128)S(1)}) custom-call(s32[6]{0:T(128)} %refs_0_.13, s32[6,5]{1,0:T(8,128)} %refs_1_.11, f32[2,8]{1,0:T(2,128)} %refs_2_.7, f32[6,5,2,128,128]{4,3,2,1,0:T(8,128)} %refs_3_.11, f32[8,2,768,128]{3,2,1,0:T(8,128)} %refs_4_.11, f32[8,128]{1,0:T(8,128)S(1)} %get-tuple-element.59.refs_5_), custom_call_target="tpu_custom_call" | custom-call | tf_op jit(solution)/shard_map/ham/pallas_call | solution.py:56
  34.0 3.8 %collective-permute-done.refs_1_ = f32[2,256,256]{2,1,0:T(8,128)S(1)} collective-permute-done((f32[2,256,256]{2,1,0:T(8,128)S(1)}, f32[2,256,256]{2,1,0:T(8,128)S(1)}, u32[]{:S(2)}, u32[]{:S(2)}) %collective-permute-start) | collective-permute-done | bytes 524320 | tf_op jit(solution)/shard_map/ppermute | solution.py:519
  37.8 0.7 collective-permute-start.4
  38.6 1.3 %collective-permute-start.10 = (f32[2,256,256]{2,1,0:T(8,128)S(1)}, f32[2,256,256]{2,1,0:T(8,128)S(1)}, u32[]{:S(2)}, u32[]{:S(2)}) collective-permute-start(f32[2,256,256]{2,1,0:T(8,128)S(1)} %get-tuple-element.76.refs_5_), channel_id=1, source_target_pairs={{4,0},{8,12},{5,1},{9,13},{6,2},{10,14},{7,3},{11,15},{20,16},{24,... | collective-permute-start | bytes 1572872 | tf_op jit(solution)/shard_map/ppermute | solution.py:519
  39.9 10.2 %collective-permute-done.5.refs_6_ = f32[2,256,256]{2,1,0:T(8,128)S(1)} collective-permute-done((f32[2,256,256]{2,1,0:T(8,128)S(1)}, f32[2,256,256]{2,1,0:T(8,128)S(1)}, u32[]{:S(2)}, u32[]{:S(2)}) %collective-permute-start.5) | collective-permute-done | bytes 524320 | tf_op jit(solution)/shard_map/ppermute | solution.py:519
  50.1 2.5 %finish.3 = (f32[8,2,768,128]{3,2,1,0:T(8,128)}, f32[2,768,256]{2,1,0:T(8,128)}, f32[8,128]{1,0:T(8,128)S(1)}) custom-call(s32[8]{0:T(128)} %refs_0_.15, s32[1]{0:T(128)} %bitcast.refs_0_.refs_1_, bf16[2,256,256]{2,1,0:T(8,128)(2,1)S(1)} %get-tuple-element.45.refs_2_, bf16[2,256,256]{2,1,0:T(8,128)(2,1)S(1)} %get-tuple-element.46.refs_3_, ...), custom_call_target="tpu_custom_call" | custom-call | flops 10000000000 | bytes 10000000000 | tf_op jit(solution)/shard_map/finish/pallas_call | solution.py:56
  52.6 6.7 %ham.5 = (f32[8,2,256,128]{3,2,1,0:T(8,128)S(1)}, f32[8,128]{1,0:T(8,128)S(1)}) custom-call(s32[6]{0:T(128)} %refs_0_.13, s32[6,5]{1,0:T(8,128)} %refs_1_.11, f32[2,8]{1,0:T(2,128)} %refs_2_.7, f32[6,5,2,128,128]{4,3,2,1,0:T(8,128)} %refs_3_.11, f32[8,2,768,128]{3,2,1,0:T(8,128)} %refs_4_.11, f32[8,128]{1,0:T(8,128)S(1)} %get-tuple-element.67.refs_5_), custom_call_target="tpu_custom_call" | custom-call | tf_op jit(solution)/shard_map/ham/pallas_call | solution.py:56
  59.4 1.3 %collective-permute-start.7 = (f32[2,256,256]{2,1,0:T(8,128)S(1)}, f32[2,256,256]{2,1,0:T(8,128)S(1)}, u32[]{:S(2)}, u32[]{:S(2)}) collective-permute-start(f32[2,256,256]{2,1,0:T(8,128)S(1)} %get-tuple-element.69.refs_5_), channel_id=1, source_target_pairs={{4,0},{8,12},{5,1},{9,13},{6,2},{10,14},{7,3},{11,15},{20,16},{24,... | collective-permute-start | bytes 1572872 | tf_op jit(solution)/shard_map/ppermute | solution.py:519
  60.7 4.4 %edge.1 = (f32[8,2,256,128]{3,2,1,0:T(8,128)S(1)}, f32[8,2,256,128]{3,2,1,0:T(8,128)S(1)}, f32[8,128]{1,0:T(8,128)S(1)}) custom-call(s32[6]{0:T(128)} %refs_0_.13, s32[6,5]{1,0:T(8,128)} %refs_1_.11, s32[1]{0:T(128)} %bitcast.1.refs_2_, f32[6,5,2,128,128]{4,3,2,1,0:T(8,128)} %refs_3_.11, f32[1,8,2,256,128]{4,3,2,1,0:T(8,128)S(1)} %bitcast.4, ...), custom_call_target="tpu_custom_call" | custom-call | tf_op jit(solution)/shard_map/edge/pallas_call | solution.py:56
  65.1 2.5 %finish.4 = (f32[8,2,768,128]{3,2,1,0:T(8,128)}, f32[2,768,256]{2,1,0:T(8,128)}, f32[8,128]{1,0:T(8,128)S(1)}) custom-call(s32[8]{0:T(128)} %refs_0_.15, s32[1]{0:T(128)} %bitcast.refs_0_.refs_1_, bf16[2,256,256]{2,1,0:T(8,128)(2,1)S(1)} %get-tuple-element.45.refs_2_, ...), custom_call_target="tpu_custom_call", output_to_operand_aliasing={{0}: (8, {}), {1}: (9, {})} | custom-call | tf_op jit(solution)/shard_map/finish/pallas_call | solution.py:56
  67.6 6.5 %collective-permute-done.7.refs_6_ = f32[2,256,256]{2,1,0:T(8,128)S(1)} collective-permute-done((f32[2,256,256]{2,1,0:T(8,128)S(1)}, f32[2,256,256]{2,1,0:T(8,128)S(1)}, u32[]{:S(2)}, u32[]{:S(2)}) %collective-permute-start.7) | collective-permute-done | bytes 524320 | tf_op jit(solution)/shard_map/ppermute | solution.py:519
  74.1 2.5 %finish.5 = (f32[8,2,768,128]{3,2,1,0:T(8,128)}, f32[2,768,256]{2,1,0:T(8,128)}, f32[8,128]{1,0:T(8,128)}) custom-call(s32[8]{0:T(128)} %refs_0_.15, s32[1]{0:T(128)} %bitcast.refs_0_.refs_1_, bf16[2,256,256]{2,1,0:T(8,128)(2,1)S(1)} %get-tuple-element.45.refs_2_, ...), custom_call_target="tpu_custom_call", output_to_operand_aliasing={{0}: (8, {}), {1}: (9, {})} | custom-call | tf_op jit(solution)/shard_map/finish/pallas_call | solution.py:56
  (18 shorter events, 0.4 us)
Async XLA Ops:
  0.6 4.1 %copy-start.1 = (f32[2,2,128,128]{3,2,1,0:T(8,128)S(1)}, f32[2,2,128,128]{3,2,1,0:T(8,128)}, u32[]{:S(2)}) copy-start(f32[2,2,128,128]{3,2,1,0:T(8,128)} %refs_3_.7) | copy-start | bytes 786436
  3.2 18.3 %collective-permute-start.1 = (f32[2,256,256]{2,1,0:T(8,128)S(1)}, f32[2,256,256]{2,1,0:T(8,128)S(1)}, u32[]{:S(2)}, u32[]{:S(2)}) collective-permute-start(f32[2,256,256]{2,1,0:T(8,128)S(1)} %get-tuple-element.49), channel_id=1, source_target_pairs={{0,4},{12,8},{1,5},{13,9},{2,6},{14,10},{3,7},{15,11},{16,20},{28,... | collective-permute-start | bytes 1572872 | tf_op jit(solution)/shard_map/ppermute | solution.py:519
  9.8 16.8 %collective-permute-start.3 = (f32[2,256,256]{2,1,0:T(8,128)S(1)}, f32[2,256,256]{2,1,0:T(8,128)S(1)}, u32[]{:S(2)}, u32[]{:S(2)}) collective-permute-start(f32[2,256,256]{2,1,0:T(8,128)S(1)} %get-tuple-element.53.refs_0_), channel_id=1, source_target_pairs={{0,4},{12,8},{1,5},{13,9},{2,6},{14,10},{3,7},{15,11},{16,20},{28,... | collective-permute-start | bytes 1572872 | tf_op jit(solution)/shard_map/ppermute | solution.py:519
  11.1 26.7 %collective-permute-start = (f32[2,256,256]{2,1,0:T(8,128)S(1)}, f32[2,256,256]{2,1,0:T(8,128)S(1)}, u32[]{:S(2)}, u32[]{:S(2)}) collective-permute-start(f32[2,256,256]{2,1,0:T(8,128)S(1)} %get-tuple-element.47.refs_0_), channel_id=1, source_target_pairs={{0,4},{12,8},{1,5},{13,9},{2,6},{14,10},{3,7},{15,11},{16,20},{28,... | collective-permute-start | bytes 1572872 | tf_op jit(solution)/shard_map/ppermute | solution.py:519
  21.6 5.7 %collective-permute-start.2 = (f32[2,256,256]{2,1,0:T(8,128)S(1)}, f32[2,256,256]{2,1,0:T(8,128)S(1)}, u32[]{:S(2)}, u32[]{:S(2)}) collective-permute-start(f32[2,256,256]{2,1,0:T(8,128)S(1)} %get-tuple-element.52.refs_0_), channel_id=1, source_target_pairs={{4,8},{8,4},{5,9},{9,5},{6,10},{10,6},{7,11},{11,7},{20,24},{24,20... | collective-permute-start | bytes 1572872 | tf_op jit(solution)/shard_map/ppermute | solution.py:519
  22.3 38.4 %collective-permute-start.8 = (f32[8,2,256,128]{3,2,1,0:T(8,128)}, f32[8,2,256,128]{3,2,1,0:T(8,128)S(1)}, u32[]{:S(2)}, u32[]{:S(2)}) collective-permute-start(f32[8,2,256,128]{3,2,1,0:T(8,128)} %get-tuple-element.70), channel_id=1, source_target_pairs={{0,1},{2,3},{1,0},{3,2},{4,5},{6,7},{5,4},{7,6},{8,9},{10,11},{9,8... | collective-permute-start | bytes 6291464 | tf_op jit(solution)/shard_map/ppermute | solution.py:553
  22.4 38.3 %collective-permute-start.9 = (f32[8,2,256,128]{3,2,1,0:T(8,128)}, f32[8,2,256,128]{3,2,1,0:T(8,128)S(1)}, u32[]{:S(2)}, u32[]{:S(2)}) collective-permute-start(f32[8,2,256,128]{3,2,1,0:T(8,128)} %get-tuple-element.71), channel_id=1, source_target_pairs={{1,2},{2,1},{5,6},{6,5},{9,10},{10,9},{13,14},{14,13},{17,18},{18,... | collective-permute-start | bytes 6291464 | tf_op jit(solution)/shard_map/ppermute | solution.py:554
  26.6 11.9 %collective-permute-start.6 = (f32[2,256,256]{2,1,0:T(8,128)S(1)}, f32[2,256,256]{2,1,0:T(8,128)S(1)}, u32[]{:S(2)}, u32[]{:S(2)}) collective-permute-start(f32[2,256,256]{2,1,0:T(8,128)S(1)} %get-tuple-element.64.refs_0_), channel_id=1, source_target_pairs={{4,8},{8,4},{5,9},{9,5},{6,10},{10,6},{7,11},{11,7},{20,24},{24,20... | collective-permute-start | bytes 1572872 | tf_op jit(solution)/shard_map/ppermute | solution.py:519
  27.4 22.7 %collective-permute-start.5 = (f32[2,256,256]{2,1,0:T(8,128)S(1)}, f32[2,256,256]{2,1,0:T(8,128)S(1)}, u32[]{:S(2)}, u32[]{:S(2)}) collective-permute-start(f32[2,256,256]{2,1,0:T(8,128)S(1)} %get-tuple-element.62.refs_5_), channel_id=1, source_target_pairs={{4,0},{8,12},{5,1},{9,13},{6,2},{10,14},{7,3},{11,15},{20,16},{24,... | collective-permute-start | bytes 1572872 | tf_op jit(solution)/shard_map/ppermute | solution.py:519
  34.0 16.1 %copy-start = (f32[2,768,256]{2,1,0:T(8,128)S(1)}, f32[2,768,256]{2,1,0:T(8,128)}, u32[]{:S(2)}) copy-start(f32[2,768,256]{2,1,0:T(8,128)} %refs_4_.13) | copy-start | bytes 4718596
  37.8 21.5 %collective-permute-start.4 = (f32[2,256,256]{2,1,0:T(8,128)S(1)}, f32[2,256,256]{2,1,0:T(8,128)S(1)}, u32[]{:S(2)}, u32[]{:S(2)}) collective-permute-start(f32[2,256,256]{2,1,0:T(8,128)S(1)} %get-tuple-element.61.refs_0_), channel_id=1, source_target_pairs={{4,8},{8,4},{5,9},{9,5},{6,10},{10,6},{7,11},{11,7},{20,24},{24,20... | collective-permute-start | bytes 1572872 | tf_op jit(solution)/shard_map/ppermute | solution.py:519
  38.6 26.5 %collective-permute-start.10 = (f32[2,256,256]{2,1,0:T(8,128)S(1)}, f32[2,256,256]{2,1,0:T(8,128)S(1)}, u32[]{:S(2)}, u32[]{:S(2)}) collective-permute-start(f32[2,256,256]{2,1,0:T(8,128)S(1)} %get-tuple-element.76.refs_5_), channel_id=1, source_target_pairs={{4,0},{8,12},{5,1},{9,13},{6,2},{10,14},{7,3},{11,15},{20,16},{24,... | collective-permute-start | bytes 1572872 | tf_op jit(solution)/shard_map/ppermute | solution.py:519
  59.4 14.7 %collective-permute-start.7 = (f32[2,256,256]{2,1,0:T(8,128)S(1)}, f32[2,256,256]{2,1,0:T(8,128)S(1)}, u32[]{:S(2)}, u32[]{:S(2)}) collective-permute-start(f32[2,256,256]{2,1,0:T(8,128)S(1)} %get-tuple-element.69.refs_5_), channel_id=1, source_target_pairs={{4,0},{8,12},{5,1},{9,13},{6,2},{10,14},{7,3},{11,15},{20,16},{24,... | collective-permute-start | bytes 1572872 | tf_op jit(solution)/shard_map/ppermute | solution.py:519
where the time goes:
time: 77.1 us; the launch traced here: 76.8 us
  Pallas kernels  40.9 us (53%)
  waiting for transfers between devices  23.8 us (31%)
  starting transfers between devices  11 us (14%)
  between operations  1.08 us (1%)
    pallas_call x16, Pallas kernels, call(): pl.pallas_call(body, in_specs=specs + [places[place] for _, place in thro...  40.9 us
    ppermute x9, waiting for transfers between devices, send(): received[c] = lax.ppermute(mine, 'pole', fold_pairs(stage))  23.8 us
    ppermute x9, starting transfers between devices, send(): received[c] = lax.ppermute(mine, 'pole', fold_pairs(stage))  10.1 us
  transfers between devices with their start and end apart: 11, of which 4 were waited for; matrix products, arithmetic and copies ran while one was open for 0% of the time, Pallas kernels for 47%

commit v1 on v0

--- a/solution.py
+++ b/solution.py
@@ -108,7 +108,7 @@
     lax.fori_loop(0, rows // tile, step, 0)
 
 
-def first_kernel(first, last, sends_ref, lead_ref, residue_ref, aux_ref, out_ref, mode_ref, sems):
+def first_kernel(first, last, axis, lead_ref, residue_ref, aux_ref, out_ref, mode_ref, lead_here, residue_here, sems, scalar_sems):
     pieces = 4
     size = (last - first) // pieces
     copies = [
@@ -119,14 +119,25 @@
         )
         for i in range(pieces)
     ]
-
-    @pl.when(sends_ref[0] == 1)
-    def _():
-        for copy in copies:
+    scalars = [
+        pltpu.make_async_copy(lead_ref, lead_here, scalar_sems.at[0]),
+        pltpu.make_async_copy(residue_ref, residue_here, scalar_sems.at[1]),
+    ]
+
+    def work():
+        for copy in scalars + copies:
             copy.start()
+        for copy in scalars:
+            copy.wait()
         for i, copy in enumerate(copies):
             copy.wait()
-            mix_range(lead_ref, residue_ref, mode_ref, out_ref, i * size, i * size, size)
+            mix_range(lead_here, residue_here, mode_ref, out_ref, i * size, i * size, size)
+
+    if axis is None:
+        work()
+    else:
+        me = lax.axis_index(axis)
+        pl.when((me == 0) | (me == lax.axis_size(axis) - 1))(work)
 
 
 def later_kernel(ranges, lead_ref, residue_ref, odd_ref, gamma_ref, aux_ref, *rest):
@@ -471,6 +482,7 @@
     line = count % 2 == 0 and count >= 4
 
     taken = ((me == 0) | (me == count - 1)).astype(jnp.int32).reshape(1)
+
     sends = taken if line else jnp.ones_like(taken)
 
     chunks = CHUNKS
@@ -479,10 +491,16 @@
     sizes = [b - a for a, b in ranges]
 
     (part,), token = call(
-        functools.partial(first_kernel, *ranges[0]), "mix",
-        [(sends, "smem"), (pole_lead, "smem"), (residues, "smem"), (aux_modes, "hbm")],
-        [((2, sizes[0], 2 * width), F32, "vmem")],
-        scratch=[pltpu.VMEM((poles, 2, sizes[0], width), F32), pltpu.SemaphoreType.DMA((4,))],
+        functools.partial(first_kernel, *ranges[0], "pole" if line else None), "mix",
+        [(pole_lead, "hbm"), (residues, "hbm"), (aux_modes, "hbm")],
+        [((2, sizes[0], 2 * width), F32, "vmem")], [sends],
+        scratch=[
+            pltpu.VMEM((poles, 2, sizes[0], width), F32),
+            pltpu.SMEM(pole_lead.shape, jnp.int32),
+            pltpu.SMEM(residues.shape, F32),
+            pltpu.SemaphoreType.DMA((4,)),
+            pltpu.SemaphoreType.DMA((2,)),
+        ],
     )
     later, token = call(
         functools.partial(later_kernel, ranges), "mix_later",

time: 77.1 us -> 74.4 us (0.965)
  the two profiles are of different devices: /device:TPU:7 before, /device:TPU:0 now
where the time goes in v1:
time: 74.4 us; the launch traced here: 74.9 us
  Pallas kernels  30.5 us (41%)
  waiting for transfers between devices  27.6 us (37%)
  starting transfers between devices  15.8 us (21%)
  between operations  1.07 us (1%)
    pallas_call x16, Pallas kernels, call(): pl.pallas_call(body, in_specs=specs + [places[place] for _, place in thro...  30.5 us
    ppermute x9, waiting for transfers between devices, send(): received[c] = lax.ppermute(mine, 'pole', fold_pairs(stage))  27.6 us
    ppermute x9, starting transfers between devices, send(): received[c] = lax.ppermute(mine, 'pole', fold_pairs(stage))  11.8 us
    ppermute x1, starting transfers between devices, neighbours(): lax.ppermute(near, 'row', near_pairs + [(b, a) for a, b in near_pairs])  3.18 us
  transfers between devices with their start and end apart: 11, of which 5 were waited for; matrix products, arithmetic and copies ran while one was open for 0% of the time, Pallas kernels for 35%

profile of v1, /device:TPU:0, one launch (start us, length us, event | category | flops | bytes accessed | tf_op | source)
XLA Modules:
  0.0 74.9 jit_solution(16942181973032091798)
XLA Ops:
  0.7 1.8 %mix.1 = (f32[2,256,256]{2,1,0:T(8,128)S(1)}, f32[8,128]{1,0:T(8,128)S(1)}) custom-call(s32[8]{0:T(128)} %refs_0_.17, f32[2,8]{1,0:T(2,128)} %refs_1_.7, f32[8,2,768,128]{3,2,1,0:T(8,128)} %refs_4_.11, s32[1]{0:T(128)} %bitcast.refs_3_.refs_1_), custom_call_target="tpu_custom_call" | custom-call | tf_op jit(solution)/shard_map/mix/pallas_call | solution.py:56
  2.5 3.2 %collective-permute-start.1 = (f32[2,256,256]{2,1,0:T(8,128)S(1)}, f32[2,256,256]{2,1,0:T(8,128)S(1)}, u32[]{:S(2)}, u32[]{:S(2)}) collective-permute-start(f32[2,256,256]{2,1,0:T(8,128)S(1)} %get-tuple-element.49), channel_id=1, source_target_pairs={{0,4},{12,8},{1,5},{13,9},{2,6},{14,10},{3,7},{15,11},{16,20},{28,... | collective-permute-start | bytes 1572872 | tf_op jit(solution)/shard_map/ppermute | solution.py:537
  5.7 5.0 %mix_later.1 = (f32[2,256,256]{2,1,0:T(8,128)S(1)}, f32[2,256,256]{2,1,0:T(8,128)S(1)}, f32[2,256,256]{2,1,0:T(8,128)S(1)}, f32[8,2,256,128]{3,2,1,0:T(8,128)}, ...) custom-call(s32[8]{0:T(128)} %refs_0_.17, ...), custom_call_target="tpu_custom_call" | custom-call | tf_op jit(solution)/shard_map/mix_later/pallas_call | solution.py:56
  10.7 1.3 %collective-permute-start.3 = (f32[2,256,256]{2,1,0:T(8,128)S(1)}, f32[2,256,256]{2,1,0:T(8,128)S(1)}, u32[]{:S(2)}, u32[]{:S(2)}) collective-permute-start(f32[2,256,256]{2,1,0:T(8,128)S(1)} %get-tuple-element.53.refs_0_), channel_id=1, source_target_pairs={{0,4},{12,8},{1,5},{13,9},{2,6},{14,10},{3,7},{15,11},{16,20},{28,... | collective-permute-start | bytes 1572872 | tf_op jit(solution)/shard_map/ppermute | solution.py:537
  12.0 1.3 %collective-permute-start = (f32[2,256,256]{2,1,0:T(8,128)S(1)}, f32[2,256,256]{2,1,0:T(8,128)S(1)}, u32[]{:S(2)}, u32[]{:S(2)}) collective-permute-start(f32[2,256,256]{2,1,0:T(8,128)S(1)} %get-tuple-element.47.refs_0_), channel_id=1, source_target_pairs={{0,4},{12,8},{1,5},{13,9},{2,6},{14,10},{3,7},{15,11},{16,20},{28,... | collective-permute-start | bytes 1572872 | tf_op jit(solution)/shard_map/ppermute | solution.py:537
  13.4 4.8 %ham.3 = (f32[8,2,256,128]{3,2,1,0:T(8,128)S(1)}, f32[8,128]{1,0:T(8,128)S(1)}) custom-call(s32[6]{0:T(128)} %refs_0_.15, s32[6,5]{1,0:T(8,128)} %refs_1_.11, f32[2,8]{1,0:T(2,128)} %refs_2_.7, f32[6,5,2,128,128]{4,3,2,1,0:T(8,128)} %refs_3_.9, f32[8,2,768,128]{3,2,1,0:T(8,128)} %refs_4_.11, f32[8,128]{1,0:T(8,128)S(1)} %get-tuple-element.50.refs_5_), custom_call_target="tpu_custom_call" | custom-call | tf_op jit(solution)/shard_map/ham/pallas_call | solution.py:56
  18.3 0.7 collective-permute-start.2
  19.0 3.2 %collective-permute-start.8 = (f32[8,2,256,128]{3,2,1,0:T(8,128)}, f32[8,2,256,128]{3,2,1,0:T(8,128)S(1)}, u32[]{:S(2)}, u32[]{:S(2)}) collective-permute-start(f32[8,2,256,128]{3,2,1,0:T(8,128)} %get-tuple-element.70), channel_id=1, source_target_pairs={{0,1},{2,3},{1,0},{3,2},{4,5},{6,7},{5,4},{7,6},{8,9},{10,11},{9,8... | collective-permute-start | bytes 6291464 | tf_op jit(solution)/shard_map/ppermute | solution.py:571
  22.2 0.8 %collective-permute-start.9 = (f32[8,2,256,128]{3,2,1,0:T(8,128)}, f32[8,2,256,128]{3,2,1,0:T(8,128)S(1)}, u32[]{:S(2)}, u32[]{:S(2)}) collective-permute-start(f32[8,2,256,128]{3,2,1,0:T(8,128)} %get-tuple-element.71), channel_id=1, source_target_pairs={{1,2},{2,1},{5,6},{6,5},{9,10},{10,9},{13,14},{14,13},{17,18},{18,... | collective-permute-start | bytes 6291464 | tf_op jit(solution)/shard_map/ppermute | solution.py:572
  23.0 6.3 %collective-permute-done.3.refs_1_ = f32[2,256,256]{2,1,0:T(8,128)S(1)} collective-permute-done((f32[2,256,256]{2,1,0:T(8,128)S(1)}, f32[2,256,256]{2,1,0:T(8,128)S(1)}, u32[]{:S(2)}, u32[]{:S(2)}) %collective-permute-start.3) | collective-permute-done | bytes 524320 | tf_op jit(solution)/shard_map/ppermute | solution.py:537
  29.3 0.7 collective-permute-start.6
  30.1 1.3 %collective-permute-start.5 = (f32[2,256,256]{2,1,0:T(8,128)S(1)}, f32[2,256,256]{2,1,0:T(8,128)S(1)}, u32[]{:S(2)}, u32[]{:S(2)}) collective-permute-start(f32[2,256,256]{2,1,0:T(8,128)S(1)} %get-tuple-element.62.refs_5_), channel_id=1, source_target_pairs={{4,0},{8,12},{5,1},{9,13},{6,2},{10,14},{7,3},{11,15},{20,16},{24,... | collective-permute-start | bytes 1572872 | tf_op jit(solution)/shard_map/ppermute | solution.py:537
  31.4 3.8 %ham.4 = (f32[8,2,256,128]{3,2,1,0:T(8,128)S(1)}, f32[8,128]{1,0:T(8,128)S(1)}) custom-call(s32[6]{0:T(128)} %refs_0_.15, s32[6,5]{1,0:T(8,128)} %refs_1_.11, f32[2,8]{1,0:T(2,128)} %refs_2_.7, f32[6,5,2,128,128]{4,3,2,1,0:T(8,128)} %refs_3_.9, f32[8,2,768,128]{3,2,1,0:T(8,128)} %refs_4_.11, f32[8,128]{1,0:T(8,128)S(1)} %get-tuple-element.59.refs_5_), custom_call_target="tpu_custom_call" | custom-call | tf_op jit(solution)/shard_map/ham/pallas_call | solution.py:56
  35.2 4.1 %collective-permute-done.refs_1_ = f32[2,256,256]{2,1,0:T(8,128)S(1)} collective-permute-done((f32[2,256,256]{2,1,0:T(8,128)S(1)}, f32[2,256,256]{2,1,0:T(8,128)S(1)}, u32[]{:S(2)}, u32[]{:S(2)}) %collective-permute-start) | collective-permute-done | bytes 524320 | tf_op jit(solution)/shard_map/ppermute | solution.py:537
  39.4 0.7 collective-permute-start.4
  40.1 1.3 %collective-permute-start.10 = (f32[2,256,256]{2,1,0:T(8,128)S(1)}, f32[2,256,256]{2,1,0:T(8,128)S(1)}, u32[]{:S(2)}, u32[]{:S(2)}) collective-permute-start(f32[2,256,256]{2,1,0:T(8,128)S(1)} %get-tuple-element.76.refs_5_), channel_id=1, source_target_pairs={{4,0},{8,12},{5,1},{9,13},{6,2},{10,14},{7,3},{11,15},{20,16},{24,... | collective-permute-start | bytes 1572872 | tf_op jit(solution)/shard_map/ppermute | solution.py:537
  41.4 8.1 %collective-permute-done.5.refs_6_ = f32[2,256,256]{2,1,0:T(8,128)S(1)} collective-permute-done((f32[2,256,256]{2,1,0:T(8,128)S(1)}, f32[2,256,256]{2,1,0:T(8,128)S(1)}, u32[]{:S(2)}, u32[]{:S(2)}) %collective-permute-start.5) | collective-permute-done | bytes 524320 | tf_op jit(solution)/shard_map/ppermute | solution.py:537
  49.6 2.5 %finish.3 = (f32[8,2,768,128]{3,2,1,0:T(8,128)}, f32[2,768,256]{2,1,0:T(8,128)}, f32[8,128]{1,0:T(8,128)S(1)}) custom-call(s32[8]{0:T(128)} %refs_0_.17, s32[1]{0:T(128)} %bitcast.refs_3_.refs_1_, bf16[2,256,256]{2,1,0:T(8,128)(2,1)S(1)} %get-tuple-element.45.refs_2_, bf16[2,256,256]{2,1,0:T(8,128)(2,1)S(1)} %get-tuple-element.46.refs_3_, ...), custom_call_target="tpu_custom_call" | custom-call | flops 10000000000 | bytes 10000000000 | tf_op jit(solution)/shard_map/finish/pallas_call | solution.py:56
  52.1 4.6 %ham.5 = (f32[8,2,256,128]{3,2,1,0:T(8,128)S(1)}, f32[8,128]{1,0:T(8,128)S(1)}) custom-call(s32[6]{0:T(128)} %refs_0_.15, s32[6,5]{1,0:T(8,128)} %refs_1_.11, f32[2,8]{1,0:T(2,128)} %refs_2_.7, f32[6,5,2,128,128]{4,3,2,1,0:T(8,128)} %refs_3_.9, f32[8,2,768,128]{3,2,1,0:T(8,128)} %refs_4_.11, f32[8,128]{1,0:T(8,128)S(1)} %get-tuple-element.67.refs_5_), custom_call_target="tpu_custom_call" | custom-call | tf_op jit(solution)/shard_map/ham/pallas_call | solution.py:56
  56.7 1.3 %collective-permute-start.7 = (f32[2,256,256]{2,1,0:T(8,128)S(1)}, f32[2,256,256]{2,1,0:T(8,128)S(1)}, u32[]{:S(2)}, u32[]{:S(2)}) collective-permute-start(f32[2,256,256]{2,1,0:T(8,128)S(1)} %get-tuple-element.69.refs_5_), channel_id=1, source_target_pairs={{4,0},{8,12},{5,1},{9,13},{6,2},{10,14},{7,3},{11,15},{20,16},{24,... | collective-permute-start | bytes 1572872 | tf_op jit(solution)/shard_map/ppermute | solution.py:537
  58.0 2.6 %edge.1 = (f32[8,2,256,128]{3,2,1,0:T(8,128)S(1)}, f32[8,2,256,128]{3,2,1,0:T(8,128)S(1)}, f32[8,128]{1,0:T(8,128)S(1)}) custom-call(s32[6]{0:T(128)} %refs_0_.15, s32[6,5]{1,0:T(8,128)} %refs_1_.11, s32[1]{0:T(128)} %bitcast.1.refs_2_, f32[6,5,2,128,128]{4,3,2,1,0:T(8,128)} %refs_3_.9, f32[1,8,2,256,128]{4,3,2,1,0:T(8,128)S(1)} %bitcast.4, ...), custom_call_target="tpu_custom_call" | custom-call | tf_op jit(solution)/shard_map/edge/pallas_call | solution.py:56
  60.8 2.5 %finish.4 = (f32[8,2,768,128]{3,2,1,0:T(8,128)}, f32[2,768,256]{2,1,0:T(8,128)}, f32[8,128]{1,0:T(8,128)S(1)}) custom-call(s32[8]{0:T(128)} %refs_0_.17, s32[1]{0:T(128)} %bitcast.refs_3_.refs_1_, bf16[2,256,256]{2,1,0:T(8,128)(2,1)S(1)} %get-tuple-element.45.refs_2_, ...), custom_call_target="tpu_custom_call", output_to_operand_aliasing={{0}: (8, {}), {1}: (9, {})} | custom-call | tf_op jit(solution)/shard_map/finish/pallas_call | solution.py:56
  63.2 9.0 %collective-permute-done.7.refs_6_ = f32[2,256,256]{2,1,0:T(8,128)S(1)} collective-permute-done((f32[2,256,256]{2,1,0:T(8,128)S(1)}, f32[2,256,256]{2,1,0:T(8,128)S(1)}, u32[]{:S(2)}, u32[]{:S(2)}) %collective-permute-start.7) | collective-permute-done | bytes 524320 | tf_op jit(solution)/shard_map/ppermute | solution.py:537
  72.3 2.5 %finish.5 = (f32[8,2,768,128]{3,2,1,0:T(8,128)}, f32[2,768,256]{2,1,0:T(8,128)}, f32[8,128]{1,0:T(8,128)}) custom-call(s32[8]{0:T(128)} %refs_0_.17, s32[1]{0:T(128)} %bitcast.refs_3_.refs_1_, bf16[2,256,256]{2,1,0:T(8,128)(2,1)S(1)} %get-tuple-element.45.refs_2_, ...), custom_call_target="tpu_custom_call", output_to_operand_aliasing={{0}: (8, {}), {1}: (9, {})} | custom-call | tf_op jit(solution)/shard_map/finish/pallas_call | solution.py:56
  (18 shorter events, 0.5 us)
Async XLA Ops:
  0.6 5.1 %copy-start.1 = (f32[2,2,128,128]{3,2,1,0:T(8,128)S(1)}, f32[2,2,128,128]{3,2,1,0:T(8,128)}, u32[]{:S(2)}) copy-start(f32[2,2,128,128]{3,2,1,0:T(8,128)} %refs_3_.5) | copy-start | bytes 786436
  2.5 15.7 %collective-permute-start.1 = (f32[2,256,256]{2,1,0:T(8,128)S(1)}, f32[2,256,256]{2,1,0:T(8,128)S(1)}, u32[]{:S(2)}, u32[]{:S(2)}) collective-permute-start(f32[2,256,256]{2,1,0:T(8,128)S(1)} %get-tuple-element.49), channel_id=1, source_target_pairs={{0,4},{12,8},{1,5},{13,9},{2,6},{14,10},{3,7},{15,11},{16,20},{28,... | collective-permute-start | bytes 1572872 | tf_op jit(solution)/shard_map/ppermute | solution.py:537
  10.7 18.5 %collective-permute-start.3 = (f32[2,256,256]{2,1,0:T(8,128)S(1)}, f32[2,256,256]{2,1,0:T(8,128)S(1)}, u32[]{:S(2)}, u32[]{:S(2)}) collective-permute-start(f32[2,256,256]{2,1,0:T(8,128)S(1)} %get-tuple-element.53.refs_0_), channel_id=1, source_target_pairs={{0,4},{12,8},{1,5},{13,9},{2,6},{14,10},{3,7},{15,11},{16,20},{28,... | collective-permute-start | bytes 1572872 | tf_op jit(solution)/shard_map/ppermute | solution.py:537
  12.0 27.3 %collective-permute-start = (f32[2,256,256]{2,1,0:T(8,128)S(1)}, f32[2,256,256]{2,1,0:T(8,128)S(1)}, u32[]{:S(2)}, u32[]{:S(2)}) collective-permute-start(f32[2,256,256]{2,1,0:T(8,128)S(1)} %get-tuple-element.47.refs_0_), channel_id=1, source_target_pairs={{0,4},{12,8},{1,5},{13,9},{2,6},{14,10},{3,7},{15,11},{16,20},{28,... | collective-permute-start | bytes 1572872 | tf_op jit(solution)/shard_map/ppermute | solution.py:537
  18.3 11.7 %collective-permute-start.2 = (f32[2,256,256]{2,1,0:T(8,128)S(1)}, f32[2,256,256]{2,1,0:T(8,128)S(1)}, u32[]{:S(2)}, u32[]{:S(2)}) collective-permute-start(f32[2,256,256]{2,1,0:T(8,128)S(1)} %get-tuple-element.52.refs_0_), channel_id=1, source_target_pairs={{4,8},{8,4},{5,9},{9,5},{6,10},{10,6},{7,11},{11,7},{20,24},{24,20... | collective-permute-start | bytes 1572872 | tf_op jit(solution)/shard_map/ppermute | solution.py:537
  19.0 39.0 %collective-permute-start.8 = (f32[8,2,256,128]{3,2,1,0:T(8,128)}, f32[8,2,256,128]{3,2,1,0:T(8,128)S(1)}, u32[]{:S(2)}, u32[]{:S(2)}) collective-permute-start(f32[8,2,256,128]{3,2,1,0:T(8,128)} %get-tuple-element.70), channel_id=1, source_target_pairs={{0,1},{2,3},{1,0},{3,2},{4,5},{6,7},{5,4},{7,6},{8,9},{10,11},{9,8... | collective-permute-start | bytes 6291464 | tf_op jit(solution)/shard_map/ppermute | solution.py:571
  22.2 35.9 %collective-permute-start.9 = (f32[8,2,256,128]{3,2,1,0:T(8,128)}, f32[8,2,256,128]{3,2,1,0:T(8,128)S(1)}, u32[]{:S(2)}, u32[]{:S(2)}) collective-permute-start(f32[8,2,256,128]{3,2,1,0:T(8,128)} %get-tuple-element.71), channel_id=1, source_target_pairs={{1,2},{2,1},{5,6},{6,5},{9,10},{10,9},{13,14},{14,13},{17,18},{18,... | collective-permute-start | bytes 6291464 | tf_op jit(solution)/shard_map/ppermute | solution.py:572
  29.3 10.8 %collective-permute-start.6 = (f32[2,256,256]{2,1,0:T(8,128)S(1)}, f32[2,256,256]{2,1,0:T(8,128)S(1)}, u32[]{:S(2)}, u32[]{:S(2)}) collective-permute-start(f32[2,256,256]{2,1,0:T(8,128)S(1)} %get-tuple-element.64.refs_0_), channel_id=1, source_target_pairs={{4,8},{8,4},{5,9},{9,5},{6,10},{10,6},{7,11},{11,7},{20,24},{24,20... | collective-permute-start | bytes 1572872 | tf_op jit(solution)/shard_map/ppermute | solution.py:537
  30.1 19.5 %collective-permute-start.5 = (f32[2,256,256]{2,1,0:T(8,128)S(1)}, f32[2,256,256]{2,1,0:T(8,128)S(1)}, u32[]{:S(2)}, u32[]{:S(2)}) collective-permute-start(f32[2,256,256]{2,1,0:T(8,128)S(1)} %get-tuple-element.62.refs_5_), channel_id=1, source_target_pairs={{4,0},{8,12},{5,1},{9,13},{6,2},{10,14},{7,3},{11,15},{20,16},{24,... | collective-permute-start | bytes 1572872 | tf_op jit(solution)/shard_map/ppermute | solution.py:537
  35.2 14.3 %copy-start = (f32[2,768,256]{2,1,0:T(8,128)S(1)}, f32[2,768,256]{2,1,0:T(8,128)}, u32[]{:S(2)}) copy-start(f32[2,768,256]{2,1,0:T(8,128)} %refs_4_.13) | copy-start | bytes 4718596
  39.4 17.3 %collective-permute-start.4 = (f32[2,256,256]{2,1,0:T(8,128)S(1)}, f32[2,256,256]{2,1,0:T(8,128)S(1)}, u32[]{:S(2)}, u32[]{:S(2)}) collective-permute-start(f32[2,256,256]{2,1,0:T(8,128)S(1)} %get-tuple-element.61.refs_0_), channel_id=1, source_target_pairs={{4,8},{8,4},{5,9},{9,5},{6,10},{10,6},{7,11},{11,7},{20,24},{24,20... | collective-permute-start | bytes 1572872 | tf_op jit(solution)/shard_map/ppermute | solution.py:537
  40.1 20.6 %collective-permute-start.10 = (f32[2,256,256]{2,1,0:T(8,128)S(1)}, f32[2,256,256]{2,1,0:T(8,128)S(1)}, u32[]{:S(2)}, u32[]{:S(2)}) collective-permute-start(f32[2,256,256]{2,1,0:T(8,128)S(1)} %get-tuple-element.76.refs_5_), channel_id=1, source_target_pairs={{4,0},{8,12},{5,1},{9,13},{6,2},{10,14},{7,3},{11,15},{20,16},{24,... | collective-permute-start | bytes 1572872 | tf_op jit(solution)/shard_map/ppermute | solution.py:537
  56.7 15.6 %collective-permute-start.7 = (f32[2,256,256]{2,1,0:T(8,128)S(1)}, f32[2,256,256]{2,1,0:T(8,128)S(1)}, u32[]{:S(2)}, u32[]{:S(2)}) collective-permute-start(f32[2,256,256]{2,1,0:T(8,128)S(1)} %get-tuple-element.69.refs_5_), channel_id=1, source_target_pairs={{4,0},{8,12},{5,1},{9,13},{6,2},{10,14},{7,3},{11,15},{20,16},{24,... | collective-permute-start | bytes 1572872 | tf_op jit(solution)/shard_map/ppermute | solution.py:537

commit v2 on v1

--- a/solution.py
+++ b/solution.py
@@ -396,32 +396,38 @@
     wide_ref[...] = lead_term
     copies = [pltpu.make_async_copy(wide_ref, lead_out_ref.at[:, at, :], sems.at[poles])]
     copies[0].start()
-    for lead in range(2):
-        columns = slice(lead * width, (lead + 1) * width)
-        pair = jnp.concatenate(
-            [
-                rho_ref[part, at, columns] + 0.25 * wide_ref[part, :, columns]
-                for part in range(2)
-            ],
-            axis=1,
-        )
-        high, low = split_high_low(pair)
-        source_ref[lead] = (
-            dot(high, ghigh_ref[lead]) + dot(high, glow_ref[lead]) + dot(low, ghigh_ref[lead])
-        )
-    for pole in range(poles):
-        lead = lead_ref[pole]
-        for slope_ref, start in zip(slope_refs, starts):
-            low_row = max(start, first)
-            high_row = min(start + slope_ref.shape[2], first + rows)
-            from_ = pl.ds(low_row - start, high_row - low_row)
-            to = pl.ds(low_row - first, high_row - low_row)
-            panel_ref[pole, 0, to, :] = slope_ref[pole, 0, from_, :] + source_ref[lead, to, width:]
-            panel_ref[pole, 1, to, :] = slope_ref[pole, 1, from_, :] - source_ref[lead, to, :width]
-        copies.append(
-            pltpu.make_async_copy(panel_ref.at[pole], out_ref.at[pole, :, at, :], sems.at[pole])
-        )
-        copies[-1].start()
+    half = rows // 2
+    for part_no in range(2):
+        begin = part_no * half
+        here = pl.ds(begin, half)
+        there = pl.ds(first + begin, half)
+        for lead in range(2):
+            columns = slice(lead * width, (lead + 1) * width)
+            pair = jnp.concatenate(
+                [rho_ref[part, there, columns] + 0.25 * wide_ref[part, here, columns] for part in range(2)],
+                axis=1,
+            )
+            high, low = split_high_low(pair)
+            source_ref[lead, here, :] = (
+                dot(high, ghigh_ref[lead]) + dot(high, glow_ref[lead]) + dot(low, ghigh_ref[lead])
+            )
+        for pole in range(poles):
+            lead = lead_ref[pole]
+            for slope_ref, start in zip(slope_refs, starts):
+                low_row = max(start, first + begin)
+                high_row = min(start + slope_ref.shape[2], first + begin + half)
+                if low_row >= high_row:
+                    continue
+                from_ = pl.ds(low_row - start, high_row - low_row)
+                to = pl.ds(low_row - first, high_row - low_row)
+                panel_ref[pole, 0, to, :] = slope_ref[pole, 0, from_, :] + source_ref[lead, to, width:]
+                panel_ref[pole, 1, to, :] = slope_ref[pole, 1, from_, :] - source_ref[lead, to, :width]
+            copies.append(
+                pltpu.make_async_copy(
+                    panel_ref.at[pole, :, here, :], out_ref.at[pole, :, there, :], sems.at[part_no * (poles + 1) + pole]
+                )
+            )
+            copies[-1].start()
     for copy in copies:
         copy.wait()
 
@@ -453,7 +459,7 @@
             pltpu.VMEM((2, rows, 2 * width), F32),
             pltpu.VMEM((2, rows, 2 * width), F32),
             pltpu.VMEM((poles, 2, rows, width), F32),
-            pltpu.SemaphoreType.DMA((poles + 1,)),
+            pltpu.SemaphoreType.DMA((2 * (poles + 1),)),
         ],
         aliases=aliases,
         cost=cost,

time: 74.4 us -> 73.9 us (level)
  waiting for transfers between devices: 27.6 us -> 26.7 us
    ppermute x9, waiting for transfers between devices: 27.6 us -> 26.7 us  [send(): received[c] = lax.ppermute(mine, 'pole', fold_pairs(stage))]
  transfers between devices with their start and end apart: 11 -> 11, of which waited for: 5 -> 5; matrix products, arithmetic and copies ran while one was open for 0% -> 0% of each run, Pallas kernels for 35% -> 36%
where the time goes in v2:
time: 73.9 us
  Pallas kernels  31.1 us (42%)
  waiting for transfers between devices  26.7 us (36%)
  starting transfers between devices  15.1 us (20%)
  between operations  1.07 us (1%)
    pallas_call x16, Pallas kernels, call(): pl.pallas_call(body, in_specs=specs + [places[place] for _, place in thro...  31.1 us
    ppermute x9, waiting for transfers between devices, send(): received[c] = lax.ppermute(mine, 'pole', fold_pairs(stage))  26.7 us
    ppermute x9, starting transfers between devices, send(): received[c] = lax.ppermute(mine, 'pole', fold_pairs(stage))  11.8 us
    ppermute x1, starting transfers between devices, neighbours(): lax.ppermute(near, 'row', near_pairs + [(b, a) for a, b in near_pairs])  2.47 us
  transfers between devices with their start and end apart: 11, of which 5 were waited for; matrix products, arithmetic and copies ran while one was open for 0% of the time, Pallas kernels for 36%

profile of v2, /device:TPU:0, one launch (start us, length us, event | category | flops | bytes accessed | tf_op | source)
XLA Modules:
  0.0 73.9 jit_solution(5833828530184354983)
XLA Ops:
  0.7 1.8 %mix.1 = (f32[2,256,256]{2,1,0:T(8,128)S(1)}, f32[8,128]{1,0:T(8,128)S(1)}) custom-call(s32[8]{0:T(128)} %refs_0_.17, f32[2,8]{1,0:T(2,128)} %refs_1_.7, f32[8,2,768,128]{3,2,1,0:T(8,128)} %refs_4_.11, s32[1]{0:T(128)} %bitcast.refs_3_.refs_1_), custom_call_target="tpu_custom_call" | custom-call | tf_op jit(solution)/shard_map/mix/pallas_call | solution.py:56
  2.5 3.2 %collective-permute-start.1 = (f32[2,256,256]{2,1,0:T(8,128)S(1)}, f32[2,256,256]{2,1,0:T(8,128)S(1)}, u32[]{:S(2)}, u32[]{:S(2)}) collective-permute-start(f32[2,256,256]{2,1,0:T(8,128)S(1)} %get-tuple-element.49), channel_id=1, source_target_pairs={{0,4},{12,8},{1,5},{13,9},{2,6},{14,10},{3,7},{15,11},{16,20},{28,... | collective-permute-start | bytes 1572872 | tf_op jit(solution)/shard_map/ppermute | solution.py:543
  5.7 5.0 %mix_later.1 = (f32[2,256,256]{2,1,0:T(8,128)S(1)}, f32[2,256,256]{2,1,0:T(8,128)S(1)}, f32[2,256,256]{2,1,0:T(8,128)S(1)}, f32[8,2,256,128]{3,2,1,0:T(8,128)}, ...) custom-call(s32[8]{0:T(128)} %refs_0_.17, ...), custom_call_target="tpu_custom_call" | custom-call | tf_op jit(solution)/shard_map/mix_later/pallas_call | solution.py:56
  10.7 1.3 %collective-permute-start.3 = (f32[2,256,256]{2,1,0:T(8,128)S(1)}, f32[2,256,256]{2,1,0:T(8,128)S(1)}, u32[]{:S(2)}, u32[]{:S(2)}) collective-permute-start(f32[2,256,256]{2,1,0:T(8,128)S(1)} %get-tuple-element.53.refs_0_), channel_id=1, source_target_pairs={{0,4},{12,8},{1,5},{13,9},{2,6},{14,10},{3,7},{15,11},{16,20},{28,... | collective-permute-start | bytes 1572872 | tf_op jit(solution)/shard_map/ppermute | solution.py:543
  12.0 1.3 %collective-permute-start = (f32[2,256,256]{2,1,0:T(8,128)S(1)}, f32[2,256,256]{2,1,0:T(8,128)S(1)}, u32[]{:S(2)}, u32[]{:S(2)}) collective-permute-start(f32[2,256,256]{2,1,0:T(8,128)S(1)} %get-tuple-element.47.refs_0_), channel_id=1, source_target_pairs={{0,4},{12,8},{1,5},{13,9},{2,6},{14,10},{3,7},{15,11},{16,20},{28,... | collective-permute-start | bytes 1572872 | tf_op jit(solution)/shard_map/ppermute | solution.py:543
  13.4 4.8 %ham.3 = (f32[8,2,256,128]{3,2,1,0:T(8,128)S(1)}, f32[8,128]{1,0:T(8,128)S(1)}) custom-call(s32[6]{0:T(128)} %refs_0_.15, s32[6,5]{1,0:T(8,128)} %refs_1_.11, f32[2,8]{1,0:T(2,128)} %refs_2_.7, f32[6,5,2,128,128]{4,3,2,1,0:T(8,128)} %refs_3_.9, f32[8,2,768,128]{3,2,1,0:T(8,128)} %refs_4_.11, f32[8,128]{1,0:T(8,128)S(1)} %get-tuple-element.50.refs_5_), custom_call_target="tpu_custom_call" | custom-call | tf_op jit(solution)/shard_map/ham/pallas_call | solution.py:56
  18.3 0.7 collective-permute-start.2
  19.0 2.5 %collective-permute-start.8 = (f32[8,2,256,128]{3,2,1,0:T(8,128)}, f32[8,2,256,128]{3,2,1,0:T(8,128)S(1)}, u32[]{:S(2)}, u32[]{:S(2)}) collective-permute-start(f32[8,2,256,128]{3,2,1,0:T(8,128)} %get-tuple-element.70), channel_id=1, source_target_pairs={{0,1},{2,3},{1,0},{3,2},{4,5},{6,7},{5,4},{7,6},{8,9},{10,11},{9,8... | collective-permute-start | bytes 6291464 | tf_op jit(solution)/shard_map/ppermute | solution.py:577
  21.5 0.8 %collective-permute-start.9 = (f32[8,2,256,128]{3,2,1,0:T(8,128)}, f32[8,2,256,128]{3,2,1,0:T(8,128)S(1)}, u32[]{:S(2)}, u32[]{:S(2)}) collective-permute-start(f32[8,2,256,128]{3,2,1,0:T(8,128)} %get-tuple-element.71), channel_id=1, source_target_pairs={{1,2},{2,1},{5,6},{6,5},{9,10},{10,9},{13,14},{14,13},{17,18},{18,... | collective-permute-start | bytes 6291464 | tf_op jit(solution)/shard_map/ppermute | solution.py:578
  22.2 7.0 %collective-permute-done.3.refs_1_ = f32[2,256,256]{2,1,0:T(8,128)S(1)} collective-permute-done((f32[2,256,256]{2,1,0:T(8,128)S(1)}, f32[2,256,256]{2,1,0:T(8,128)S(1)}, u32[]{:S(2)}, u32[]{:S(2)}) %collective-permute-start.3) | collective-permute-done | bytes 524320 | tf_op jit(solution)/shard_map/ppermute | solution.py:543
  29.3 0.7 collective-permute-start.6
  30.1 1.3 %collective-permute-start.5 = (f32[2,256,256]{2,1,0:T(8,128)S(1)}, f32[2,256,256]{2,1,0:T(8,128)S(1)}, u32[]{:S(2)}, u32[]{:S(2)}) collective-permute-start(f32[2,256,256]{2,1,0:T(8,128)S(1)} %get-tuple-element.62.refs_5_), channel_id=1, source_target_pairs={{4,0},{8,12},{5,1},{9,13},{6,2},{10,14},{7,3},{11,15},{20,16},{24,... | collective-permute-start | bytes 1572872 | tf_op jit(solution)/shard_map/ppermute | solution.py:543
  31.4 4.5 %ham.4 = (f32[8,2,256,128]{3,2,1,0:T(8,128)S(1)}, f32[8,128]{1,0:T(8,128)S(1)}) custom-call(s32[6]{0:T(128)} %refs_0_.15, s32[6,5]{1,0:T(8,128)} %refs_1_.11, f32[2,8]{1,0:T(2,128)} %refs_2_.7, f32[6,5,2,128,128]{4,3,2,1,0:T(8,128)} %refs_3_.9, f32[8,2,768,128]{3,2,1,0:T(8,128)} %refs_4_.11, f32[8,128]{1,0:T(8,128)S(1)} %get-tuple-element.59.refs_5_), custom_call_target="tpu_custom_call" | custom-call | tf_op jit(solution)/shard_map/ham/pallas_call | solution.py:56
  35.9 3.4 %collective-permute-done.refs_1_ = f32[2,256,256]{2,1,0:T(8,128)S(1)} collective-permute-done((f32[2,256,256]{2,1,0:T(8,128)S(1)}, f32[2,256,256]{2,1,0:T(8,128)S(1)}, u32[]{:S(2)}, u32[]{:S(2)}) %collective-permute-start) | collective-permute-done | bytes 524320 | tf_op jit(solution)/shard_map/ppermute | solution.py:543
  39.4 0.7 collective-permute-start.4
  40.1 1.3 %collective-permute-start.10 = (f32[2,256,256]{2,1,0:T(8,128)S(1)}, f32[2,256,256]{2,1,0:T(8,128)S(1)}, u32[]{:S(2)}, u32[]{:S(2)}) collective-permute-start(f32[2,256,256]{2,1,0:T(8,128)S(1)} %get-tuple-element.76.refs_5_), channel_id=1, source_target_pairs={{4,0},{8,12},{5,1},{9,13},{6,2},{10,14},{7,3},{11,15},{20,16},{24,... | collective-permute-start | bytes 1572872 | tf_op jit(solution)/shard_map/ppermute | solution.py:543
  41.4 6.6 %collective-permute-done.5.refs_6_ = f32[2,256,256]{2,1,0:T(8,128)S(1)} collective-permute-done((f32[2,256,256]{2,1,0:T(8,128)S(1)}, f32[2,256,256]{2,1,0:T(8,128)S(1)}, u32[]{:S(2)}, u32[]{:S(2)}) %collective-permute-start.5) | collective-permute-done | bytes 524320 | tf_op jit(solution)/shard_map/ppermute | solution.py:543
  48.0 2.5 %finish.3 = (f32[8,2,768,128]{3,2,1,0:T(8,128)}, f32[2,768,256]{2,1,0:T(8,128)}, f32[8,128]{1,0:T(8,128)S(1)}) custom-call(s32[8]{0:T(128)} %refs_0_.17, s32[1]{0:T(128)} %bitcast.refs_3_.refs_1_, bf16[2,256,256]{2,1,0:T(8,128)(2,1)S(1)} %get-tuple-element.45.refs_2_, bf16[2,256,256]{2,1,0:T(8,128)(2,1)S(1)} %get-tuple-element.46.refs_3_, ...), custom_call_target="tpu_custom_call" | custom-call | flops 10000000000 | bytes 10000000000 | tf_op jit(solution)/shard_map/finish/pallas_call | solution.py:56
  50.5 4.5 %ham.5 = (f32[8,2,256,128]{3,2,1,0:T(8,128)S(1)}, f32[8,128]{1,0:T(8,128)S(1)}) custom-call(s32[6]{0:T(128)} %refs_0_.15, s32[6,5]{1,0:T(8,128)} %refs_1_.11, f32[2,8]{1,0:T(2,128)} %refs_2_.7, f32[6,5,2,128,128]{4,3,2,1,0:T(8,128)} %refs_3_.9, f32[8,2,768,128]{3,2,1,0:T(8,128)} %refs_4_.11, f32[8,128]{1,0:T(8,128)S(1)} %get-tuple-element.67.refs_5_), custom_call_target="tpu_custom_call" | custom-call | tf_op jit(solution)/shard_map/ham/pallas_call | solution.py:56
  55.2 1.3 %collective-permute-start.7 = (f32[2,256,256]{2,1,0:T(8,128)S(1)}, f32[2,256,256]{2,1,0:T(8,128)S(1)}, u32[]{:S(2)}, u32[]{:S(2)}) collective-permute-start(f32[2,256,256]{2,1,0:T(8,128)S(1)} %get-tuple-element.69.refs_5_), channel_id=1, source_target_pairs={{4,0},{8,12},{5,1},{9,13},{6,2},{10,14},{7,3},{11,15},{20,16},{24,... | collective-permute-start | bytes 1572872 | tf_op jit(solution)/shard_map/ppermute | solution.py:543
  56.5 2.5 %edge.1 = (f32[8,2,256,128]{3,2,1,0:T(8,128)S(1)}, f32[8,2,256,128]{3,2,1,0:T(8,128)S(1)}, f32[8,128]{1,0:T(8,128)S(1)}) custom-call(s32[6]{0:T(128)} %refs_0_.15, s32[6,5]{1,0:T(8,128)} %refs_1_.11, s32[1]{0:T(128)} %bitcast.1.refs_2_, f32[6,5,2,128,128]{4,3,2,1,0:T(8,128)} %refs_3_.9, f32[1,8,2,256,128]{4,3,2,1,0:T(8,128)S(1)} %bitcast.4, ...), custom_call_target="tpu_custom_call" | custom-call | tf_op jit(solution)/shard_map/edge/pallas_call | solution.py:56
  59.2 2.5 %finish.4 = (f32[8,2,768,128]{3,2,1,0:T(8,128)}, f32[2,768,256]{2,1,0:T(8,128)}, f32[8,128]{1,0:T(8,128)S(1)}) custom-call(s32[8]{0:T(128)} %refs_0_.17, s32[1]{0:T(128)} %bitcast.refs_3_.refs_1_, bf16[2,256,256]{2,1,0:T(8,128)(2,1)S(1)} %get-tuple-element.45.refs_2_, ...), custom_call_target="tpu_custom_call", output_to_operand_aliasing={{0}: (8, {}), {1}: (9, {})} | custom-call | tf_op jit(solution)/shard_map/finish/pallas_call | solution.py:56
  61.8 9.5 %collective-permute-done.7.refs_6_ = f32[2,256,256]{2,1,0:T(8,128)S(1)} collective-permute-done((f32[2,256,256]{2,1,0:T(8,128)S(1)}, f32[2,256,256]{2,1,0:T(8,128)S(1)}, u32[]{:S(2)}, u32[]{:S(2)}) %collective-permute-start.7) | collective-permute-done | bytes 524320 | tf_op jit(solution)/shard_map/ppermute | solution.py:543
  71.2 2.5 %finish.5 = (f32[8,2,768,128]{3,2,1,0:T(8,128)}, f32[2,768,256]{2,1,0:T(8,128)}, f32[8,128]{1,0:T(8,128)}) custom-call(s32[8]{0:T(128)} %refs_0_.17, s32[1]{0:T(128)} %bitcast.refs_3_.refs_1_, bf16[2,256,256]{2,1,0:T(8,128)(2,1)S(1)} %get-tuple-element.45.refs_2_, ...), custom_call_target="tpu_custom_call", output_to_operand_aliasing={{0}: (8, {}), {1}: (9, {})} | custom-call | tf_op jit(solution)/shard_map/finish/pallas_call | solution.py:56
  (18 shorter events, 0.7 us)
Async XLA Ops:
  0.6 5.1 %copy-start.1 = (f32[2,2,128,128]{3,2,1,0:T(8,128)S(1)}, f32[2,2,128,128]{3,2,1,0:T(8,128)}, u32[]{:S(2)}) copy-start(f32[2,2,128,128]{3,2,1,0:T(8,128)} %refs_3_.5) | copy-start | bytes 786436
  2.5 15.7 %collective-permute-start.1 = (f32[2,256,256]{2,1,0:T(8,128)S(1)}, f32[2,256,256]{2,1,0:T(8,128)S(1)}, u32[]{:S(2)}, u32[]{:S(2)}) collective-permute-start(f32[2,256,256]{2,1,0:T(8,128)S(1)} %get-tuple-element.49), channel_id=1, source_target_pairs={{0,4},{12,8},{1,5},{13,9},{2,6},{14,10},{3,7},{15,11},{16,20},{28,... | collective-permute-start | bytes 1572872 | tf_op jit(solution)/shard_map/ppermute | solution.py:543
  10.7 18.5 %collective-permute-start.3 = (f32[2,256,256]{2,1,0:T(8,128)S(1)}, f32[2,256,256]{2,1,0:T(8,128)S(1)}, u32[]{:S(2)}, u32[]{:S(2)}) collective-permute-start(f32[2,256,256]{2,1,0:T(8,128)S(1)} %get-tuple-element.53.refs_0_), channel_id=1, source_target_pairs={{0,4},{12,8},{1,5},{13,9},{2,6},{14,10},{3,7},{15,11},{16,20},{28,... | collective-permute-start | bytes 1572872 | tf_op jit(solution)/shard_map/ppermute | solution.py:543
  12.0 27.3 %collective-permute-start = (f32[2,256,256]{2,1,0:T(8,128)S(1)}, f32[2,256,256]{2,1,0:T(8,128)S(1)}, u32[]{:S(2)}, u32[]{:S(2)}) collective-permute-start(f32[2,256,256]{2,1,0:T(8,128)S(1)} %get-tuple-element.47.refs_0_), channel_id=1, source_target_pairs={{0,4},{12,8},{1,5},{13,9},{2,6},{14,10},{3,7},{15,11},{16,20},{28,... | collective-permute-start | bytes 1572872 | tf_op jit(solution)/shard_map/ppermute | solution.py:543
  18.3 11.7 %collective-permute-start.2 = (f32[2,256,256]{2,1,0:T(8,128)S(1)}, f32[2,256,256]{2,1,0:T(8,128)S(1)}, u32[]{:S(2)}, u32[]{:S(2)}) collective-permute-start(f32[2,256,256]{2,1,0:T(8,128)S(1)} %get-tuple-element.52.refs_0_), channel_id=1, source_target_pairs={{4,8},{8,4},{5,9},{9,5},{6,10},{10,6},{7,11},{11,7},{20,24},{24,20... | collective-permute-start | bytes 1572872 | tf_op jit(solution)/shard_map/ppermute | solution.py:543
  19.0 37.5 %collective-permute-start.8 = (f32[8,2,256,128]{3,2,1,0:T(8,128)}, f32[8,2,256,128]{3,2,1,0:T(8,128)S(1)}, u32[]{:S(2)}, u32[]{:S(2)}) collective-permute-start(f32[8,2,256,128]{3,2,1,0:T(8,128)} %get-tuple-element.70), channel_id=1, source_target_pairs={{0,1},{2,3},{1,0},{3,2},{4,5},{6,7},{5,4},{7,6},{8,9},{10,11},{9,8... | collective-permute-start | bytes 6291464 | tf_op jit(solution)/shard_map/ppermute | solution.py:577
  21.5 35.0 %collective-permute-start.9 = (f32[8,2,256,128]{3,2,1,0:T(8,128)}, f32[8,2,256,128]{3,2,1,0:T(8,128)S(1)}, u32[]{:S(2)}, u32[]{:S(2)}) collective-permute-start(f32[8,2,256,128]{3,2,1,0:T(8,128)} %get-tuple-element.71), channel_id=1, source_target_pairs={{1,2},{2,1},{5,6},{6,5},{9,10},{10,9},{13,14},{14,13},{17,18},{18,... | collective-permute-start | bytes 6291464 | tf_op jit(solution)/shard_map/ppermute | solution.py:578
  29.3 10.8 %collective-permute-start.6 = (f32[2,256,256]{2,1,0:T(8,128)S(1)}, f32[2,256,256]{2,1,0:T(8,128)S(1)}, u32[]{:S(2)}, u32[]{:S(2)}) collective-permute-start(f32[2,256,256]{2,1,0:T(8,128)S(1)} %get-tuple-element.64.refs_0_), channel_id=1, source_target_pairs={{4,8},{8,4},{5,9},{9,5},{6,10},{10,6},{7,11},{11,7},{20,24},{24,20... | collective-permute-start | bytes 1572872 | tf_op jit(solution)/shard_map/ppermute | solution.py:543
  30.1 17.9 %collective-permute-start.5 = (f32[2,256,256]{2,1,0:T(8,128)S(1)}, f32[2,256,256]{2,1,0:T(8,128)S(1)}, u32[]{:S(2)}, u32[]{:S(2)}) collective-permute-start(f32[2,256,256]{2,1,0:T(8,128)S(1)} %get-tuple-element.62.refs_5_), channel_id=1, source_target_pairs={{4,0},{8,12},{5,1},{9,13},{6,2},{10,14},{7,3},{11,15},{20,16},{24,... | collective-permute-start | bytes 1572872 | tf_op jit(solution)/shard_map/ppermute | solution.py:543
  35.9 12.1 %copy-start = (f32[2,768,256]{2,1,0:T(8,128)S(1)}, f32[2,768,256]{2,1,0:T(8,128)}, u32[]{:S(2)}) copy-start(f32[2,768,256]{2,1,0:T(8,128)} %refs_4_.13) | copy-start | bytes 4718596
  39.4 15.7 %collective-permute-start.4 = (f32[2,256,256]{2,1,0:T(8,128)S(1)}, f32[2,256,256]{2,1,0:T(8,128)S(1)}, u32[]{:S(2)}, u32[]{:S(2)}) collective-permute-start(f32[2,256,256]{2,1,0:T(8,128)S(1)} %get-tuple-element.61.refs_0_), channel_id=1, source_target_pairs={{4,8},{8,4},{5,9},{9,5},{6,10},{10,6},{7,11},{11,7},{20,24},{24,20... | collective-permute-start | bytes 1572872 | tf_op jit(solution)/shard_map/ppermute | solution.py:543
  40.1 19.1 %collective-permute-start.10 = (f32[2,256,256]{2,1,0:T(8,128)S(1)}, f32[2,256,256]{2,1,0:T(8,128)S(1)}, u32[]{:S(2)}, u32[]{:S(2)}) collective-permute-start(f32[2,256,256]{2,1,0:T(8,128)S(1)} %get-tuple-element.76.refs_5_), channel_id=1, source_target_pairs={{4,0},{8,12},{5,1},{9,13},{6,2},{10,14},{7,3},{11,15},{20,16},{24,... | collective-permute-start | bytes 1572872 | tf_op jit(solution)/shard_map/ppermute | solution.py:543
  55.2 16.1 %collective-permute-start.7 = (f32[2,256,256]{2,1,0:T(8,128)S(1)}, f32[2,256,256]{2,1,0:T(8,128)S(1)}, u32[]{:S(2)}, u32[]{:S(2)}) collective-permute-start(f32[2,256,256]{2,1,0:T(8,128)S(1)} %get-tuple-element.69.refs_5_), channel_id=1, source_target_pairs={{4,0},{8,12},{5,1},{9,13},{6,2},{10,14},{7,3},{11,15},{20,16},{24,... | collective-permute-start | bytes 1572872 | tf_op jit(solution)/shard_map/ppermute | solution.py:543
